TPU v7x, 512 devices: a whole 4x8x8 slice. The times are simulated.
512 devices in a mesh: tm: 128 (over z, y, core), swath: 4 (over x).
Axes of the slice: x: 4, y: 8, z: 8, core: 2. Of those that a mesh axis runs over, the one named last changes fastest.
Arguments:
- design: bfloat16 [128, 2048, 512], P('tm', 'swath'), may hold values from -6 to 6
- process: bfloat16 [128, 512, 512], P('tm', 'swath')
- prior_prec: float32 [128, 512], P('tm', 'swath'), may hold values from 0.05 to 0.5
- routes: int32 [128, 16], P('tm', 'swath'), may hold values from -1 to 127, as said below
- counts: int32 [128, 4], P('tm', 'swath'), may hold values from 1 to 4
Outputs:
- reduced_diag: float32 [128, 512, 512], P('tm', 'swath')
- reduced_coupling: float32 [128, 512, 512], P('tm', 'swath')
Inputs may be any that keep to these rules, and one draw needn't show every extreme that they name: `routes`: each value is the holder's own time block i or i + 1, or -1 only where i + 1 would be 128; of one holder's 4 blocks, exactly 2 name i and the others i + 1 or -1.
All inputs are finite; a program needn't handle non-finite values.
Results may differ from a plain program's by a relative error of at most 0.00073.
Values may be sent and summed in bfloat16 or wider, within the bound.
No kernel may reach another device: no remote copies, remote signals or barrier semaphores. Data moves between devices by JAX's collectives and lax.ppermute only.
A program may use at most 64 MiB of HBM per device.

v0:
```python
import jax
import jax.numpy as jnp
from jax import lax
from jax.sharding import PartitionSpec as P

LEVELS = 3


def passed_along(block, axis, distance):
    devices = range(lax.axis_size(axis))
    route = [(i - distance, i) for i in devices if i - distance in devices]
    return lax.ppermute(block, axis, route)


def tri_solve(factor, right):
    return lax.linalg.triangular_solve(factor, right, left_side=True, lower=True)


def inner_rows(left_side, right_side):
    return lax.dot_general(
        left_side,
        right_side,
        (((0,), (0,)), ((), ())),
        precision=lax.Precision.HIGHEST,
        preferred_element_type=jnp.float32,
    )


def compact(scaled, wanted, slot_count):
    sort_key = jnp.where(wanted, 0, 1).astype(jnp.int32)
    picked = jnp.argsort(sort_key, stable=True)[:slot_count]
    kept = jnp.take(sort_key, picked) == 0
    return jnp.where(kept[:, None, None], scaled[picked], 0.0).astype(jnp.bfloat16)


def shards(design, process, prior_prec, routes, counts):
    row_count = process.shape[1]
    order_size = process.shape[2]
    time_count = lax.axis_size("tm")
    my_time = lax.axis_index("tm")
    swath_index = lax.axis_index("swath")
    block_count = routes.shape[1]
    slot_count = block_count // 2
    block_rows = design.shape[1] // block_count
    total_slots = 2 * slot_count * block_rows * lax.axis_size("swath")
    row_start = swath_index * row_count
    raw_rows = design[0].reshape(block_count, block_rows, order_size).astype(jnp.float32)
    mean_sq = jnp.mean(raw_rows * raw_rows, axis=-1, keepdims=True)
    scaled = raw_rows * lax.rsqrt(4.0 * total_slots * (mean_sq + 1e-06))
    live = jnp.arange(block_count) < counts[0, 0]
    target = routes[0]
    own_blocks = compact(scaled, live & (target == my_time), slot_count)
    ahead_blocks = compact(scaled, live & (target == my_time + 1), slot_count)
    incoming, previous = passed_along((ahead_blocks, process), "tm", 1)
    gram_input = jnp.concatenate([own_blocks, incoming], axis=0).reshape(-1, order_size)
    shard_rows = lax.all_gather(gram_input, "swath", axis=0, tiled=True)
    columns = lax.dynamic_slice_in_dim(shard_rows, row_start, row_count, 1)
    gram = lax.dot_general(
        columns, shard_rows, (((0,), (0,)), ((), ())), preferred_element_type=jnp.float32
    )
    unit_rows = jnp.arange(order_size)[None, :] == jnp.arange(row_count)[:, None] + row_start
    diag_rows = previous[0].astype(jnp.float32) + process[0].astype(jnp.float32) + gram
    diag_rows = diag_rows + jnp.where(unit_rows, prior_prec[0][:, None], 0.0)
    coup_rows = -process[0].astype(jnp.float32)
    unit_full = jnp.eye(order_size, dtype=jnp.float32)
    for level in range(LEVELS):
        distance = 2**level
        full_diag, full_coup = (
            lax.all_gather(diag_rows, "swath", axis=0, tiled=True),
            lax.all_gather(coup_rows, "swath", axis=0, tiled=True),
        )
        factor = jnp.linalg.cholesky(full_diag)
        solved = tri_solve(factor, full_coup)
        own_cols = lax.dynamic_slice_in_dim(solved, row_start, row_count, 1)
        eliminated = inner_rows(own_cols, solved)
        left_term = passed_along(eliminated, "tm", distance)
        far_factor, far_solved = passed_along((factor, solved), "tm", -distance)
        has_partner = my_time + distance < time_count
        far_factor = jnp.where(has_partner, far_factor, unit_full)
        cross = tri_solve(far_factor, full_coup.T)
        cross_cols = lax.dynamic_slice_in_dim(cross, row_start, row_count, 1)
        right_term = inner_rows(cross_cols, cross)
        new_coupling = inner_rows(cross_cols, far_solved)
        diag_rows = diag_rows - left_term - jnp.where(has_partner, right_term, 0.0)
        coup_rows = -new_coupling
    return (diag_rows[None], coup_rows[None])


def solution(mesh):
    return jax.shard_map(
        shards,
        mesh=mesh,
        in_specs=(
            P("tm", "swath", None),
            P("tm", "swath", None),
            P("tm", "swath"),
            P("tm", "swath"),
            P("tm", "swath"),
        ),
        out_specs=(P("tm", "swath", None), P("tm", "swath", None)),
        check_vma=False,
    )
```

profile of v0, /device:TPU:20, one launch (start us, length us, event | category | flops | bytes accessed | tf_op | source)
XLA Modules:
  0.0 881.8 jit_solution(11233047935860242572)
XLA Ops:
  17.1 4.4 collective-permute-done.1
  24.6 4.3 collective-permute-done
  28.9 34.3 %all-gather.9.cloned.1.call-done = bf16[2048,512]{1,0:T(8,128)(2,1)} async-done(((bf16[512,512]{1,0:T(8,128)(2,1)}), bf16[2048,512]{1,0:T(8,128)(2,1)}) %all-gather.9.cloned.1.call-update) | async-done | bytes 2097168 | tf_op jit(solution)/shard_map/all_gather | solution.py:56
  63.2 3.3 fusion.71
  67.4 31.5 %all-gather.11.cloned.1.call-done = f32[512,512]{0,1:T(8,128)} async-done(((f32[128,512]{0,1:T(8,128)}), f32[512,512]{0,1:T(8,128)}) %all-gather.11.cloned.1.call-update) | async-done | bytes 1048592 | tf_op jit(solution)/shard_map/all_gather | solution.py:69
  100.8 11.7 %cholesky.374 = f32[128,128]{1,0:T(8,128)S(1)} custom-call(f32[128,128]{1,0:T(8,128)S(1)} %cholesky.586), custom_call_target="Cholesky" | custom-call | tf_op jit(solution)/shard_map/jit(cholesky)/cholesky | solution.py:72
  112.7 9.8 %custom-call.34 = f32[1,128,128]{1,2,0:T(8,128)S(1)} custom-call(f32[1,128,128]{2,1,0:T(8,128)S(1)} %get-tuple-element.152), custom_call_target="InvertDiagBlocksLowerTriangular" | custom-call | tf_op jit(solution)/shard_map/jit(cholesky)/cholesky | solution.py:72
  123.2 11.7 %cholesky.393 = f32[128,128]{1,0:T(8,128)S(1)} custom-call(f32[128,128]{1,0:T(8,128)S(1)} %cholesky.590), custom_call_target="Cholesky" | custom-call | tf_op jit(solution)/shard_map/jit(cholesky)/cholesky | solution.py:72
  134.9 10.2 %custom-call.35 = f32[1,128,128]{1,2,0:T(8,128)S(1)} custom-call(f32[1,128,128]{2,1,0:T(8,128)S(1)} %get-tuple-element.149), custom_call_target="InvertDiagBlocksLowerTriangular" | custom-call | tf_op jit(solution)/shard_map/jit(cholesky)/cholesky | solution.py:72
  145.8 11.7 %cholesky.414 = f32[128,128]{1,0:T(8,128)S(1)} custom-call(f32[128,128]{1,0:T(8,128)S(1)} %cholesky.595), custom_call_target="Cholesky" | custom-call | tf_op jit(solution)/shard_map/jit(cholesky)/cholesky | solution.py:72
  157.6 9.8 %custom-call.36 = f32[1,128,128]{1,2,0:T(8,128)S(1)} custom-call(f32[1,128,128]{2,1,0:T(8,128)S(1)} %get-tuple-element.146), custom_call_target="InvertDiagBlocksLowerTriangular" | custom-call | tf_op jit(solution)/shard_map/jit(cholesky)/cholesky | solution.py:72
  168.0 11.7 %cholesky.431 = f32[128,128]{1,0:T(8,128)S(1)} custom-call(f32[128,128]{1,0:T(8,128)S(1)} %convolution_subtract_fusion.14), custom_call_target="Cholesky" | custom-call | tf_op jit(solution)/shard_map/jit(cholesky)/cholesky | solution.py:72
  185.2 7.5 while.12
  192.7 39.3 %custom-call.37 = f32[4,128,128]{1,2,0:T(8,128)S(1)} custom-call(f32[4,128,128]{2,1,0:T(8,128)S(1)} %get-tuple-element.47), custom_call_target="InvertDiagBlocksLowerTriangular" | custom-call | tf_op jit(solution)/shard_map/triangular_solve/custom-call.3 | solution.py:16
  245.8 4.9 collective-permute-done.3
  251.6 10.2 %while.13 = (s32[]{:T(128)}, f32[512,512]{1,0:T(8,128)S(1)}, s32[4,2]{0,1:T(2,128)S(1)}, f32[4,128,128]{2,1,0:T(8,128)}, s32[]{:T(128)}) while((s32[]{:T(128)}, f32[512,512]{1,0:T(8,128)S(1)}, s32[4,2]{0,1:T(2,128)S(1)}, f32[4,128,128]{2,1,0:T(8,128)}, s32[]{:T(128)}) %tuple.157), condition=%wide.while_cond.clone, body=%wide.while_body.clone.sunk | while | flops 2 | bytes 132205 | solution.py:16
  261.9 40.7 %custom-call.38 = f32[4,128,128]{1,2,0:T(8,128)} custom-call(f32[4,128,128]{2,1,0:T(8,128)} %get-tuple-element.48), custom_call_target="InvertDiagBlocksLowerTriangular" | custom-call | tf_op jit(solution)/shard_map/triangular_solve/custom-call.3 | solution.py:16
  310.3 3.8 collective-permute-start.4
  314.1 12.3 %collective-permute-done.4 = f32[512,512]{1,0:T(8,128)S(1)} collective-permute-done((f32[512,512]{1,0:T(8,128)S(1)}, f32[512,512]{1,0:T(8,128)S(1)}, u32[]{:S(2)}, u32[]{:S(2)}) %collective-permute-start.4) | collective-permute-done | bytes 1048608 | tf_op jit(solution)/shard_map/ppermute | solution.py:12
  328.4 15.0 %all-gather.13.cloned.1.call-done = f32[512,512]{0,1:T(8,128)} async-done(((f32[128,512]{0,1:T(8,128)}), f32[512,512]{0,1:T(8,128)}) %all-gather.13.cloned.1.call-update) | async-done | bytes 1048592 | tf_op jit(solution)/shard_map/all_gather | solution.py:69
  345.3 11.7 %cholesky.446 = f32[128,128]{1,0:T(8,128)S(1)} custom-call(f32[128,128]{1,0:T(8,128)S(1)} %cholesky.599), custom_call_target="Cholesky" | custom-call | tf_op jit(solution)/shard_map/jit(cholesky)/cholesky | solution.py:72
  357.2 9.8 %custom-call.39 = f32[1,128,128]{1,2,0:T(8,128)S(1)} custom-call(f32[1,128,128]{2,1,0:T(8,128)S(1)} %get-tuple-element.142), custom_call_target="InvertDiagBlocksLowerTriangular" | custom-call | tf_op jit(solution)/shard_map/jit(cholesky)/cholesky | solution.py:72
  367.7 11.7 %cholesky.465 = f32[128,128]{1,0:T(8,128)S(1)} custom-call(f32[128,128]{1,0:T(8,128)S(1)} %cholesky.603), custom_call_target="Cholesky" | custom-call | tf_op jit(solution)/shard_map/jit(cholesky)/cholesky | solution.py:72
  379.4 10.0 %custom-call.40 = f32[1,128,128]{1,2,0:T(8,128)S(1)} custom-call(f32[1,128,128]{2,1,0:T(8,128)S(1)} %get-tuple-element.139), custom_call_target="InvertDiagBlocksLowerTriangular" | custom-call | tf_op jit(solution)/shard_map/jit(cholesky)/cholesky | solution.py:72
  390.0 11.7 %cholesky.486 = f32[128,128]{1,0:T(8,128)S(1)} custom-call(f32[128,128]{1,0:T(8,128)S(1)} %cholesky.608), custom_call_target="Cholesky" | custom-call | tf_op jit(solution)/shard_map/jit(cholesky)/cholesky | solution.py:72
  401.8 9.8 %custom-call.41 = f32[1,128,128]{1,2,0:T(8,128)S(1)} custom-call(f32[1,128,128]{2,1,0:T(8,128)S(1)} %get-tuple-element.136), custom_call_target="InvertDiagBlocksLowerTriangular" | custom-call | tf_op jit(solution)/shard_map/jit(cholesky)/cholesky | solution.py:72
  412.2 11.7 %cholesky.503 = f32[128,128]{1,0:T(8,128)S(1)} custom-call(f32[128,128]{1,0:T(8,128)S(1)} %convolution_subtract_fusion.13), custom_call_target="Cholesky" | custom-call | tf_op jit(solution)/shard_map/jit(cholesky)/cholesky | solution.py:72
  429.4 7.5 while.14
  437.0 39.3 %custom-call.42 = f32[4,128,128]{1,2,0:T(8,128)S(1)} custom-call(f32[4,128,128]{2,1,0:T(8,128)S(1)} %get-tuple-element.49), custom_call_target="InvertDiagBlocksLowerTriangular" | custom-call | tf_op jit(solution)/shard_map/triangular_solve/custom-call.3 | solution.py:16
  486.6 3.8 collective-permute-start.5
  490.4 15.5 %collective-permute-done.6 = f32[512,512]{1,0:T(8,128)S(1)} collective-permute-done((f32[512,512]{1,0:T(8,128)S(1)}, f32[512,512]{1,0:T(8,128)S(1)}, u32[]{:S(2)}, u32[]{:S(2)}) %collective-permute-start.6) | collective-permute-done | bytes 1048608 | tf_op jit(solution)/shard_map/ppermute | solution.py:12
  506.8 10.2 %while.15 = (s32[]{:T(128)}, f32[512,512]{1,0:T(8,128)S(1)}, s32[4,2]{0,1:T(2,128)S(1)}, f32[4,128,128]{2,1,0:T(8,128)}, s32[]{:T(128)}) while((s32[]{:T(128)}, f32[512,512]{1,0:T(8,128)S(1)}, s32[4,2]{0,1:T(2,128)S(1)}, f32[4,128,128]{2,1,0:T(8,128)}, s32[]{:T(128)}) %tuple.159), condition=%wide.while_cond.clone.2, body=%wide.while_body.clone.2.sunk | while | flops 2 | bytes 132205 | solution.py:16
  517.0 40.7 %custom-call.43 = f32[4,128,128]{1,2,0:T(8,128)} custom-call(f32[4,128,128]{2,1,0:T(8,128)} %get-tuple-element.50), custom_call_target="InvertDiagBlocksLowerTriangular" | custom-call | tf_op jit(solution)/shard_map/triangular_solve/custom-call.3 | solution.py:16
  569.7 23.4 %collective-permute-done.7 = f32[512,512]{1,0:T(8,128)S(1)} collective-permute-done((f32[512,512]{1,0:T(8,128)S(1)}, f32[512,512]{1,0:T(8,128)S(1)}, u32[]{:S(2)}, u32[]{:S(2)}) %collective-permute-start.7) | collective-permute-done | bytes 1048608 | tf_op jit(solution)/shard_map/ppermute | solution.py:12
  594.6 4.8 all-gather.17.cloned.1.call-done
  601.3 11.7 %cholesky.518 = f32[128,128]{1,0:T(8,128)S(1)} custom-call(f32[128,128]{1,0:T(8,128)S(1)} %cholesky.612), custom_call_target="Cholesky" | custom-call | tf_op jit(solution)/shard_map/jit(cholesky)/cholesky | solution.py:72
  613.2 9.8 %custom-call.44 = f32[1,128,128]{1,2,0:T(8,128)S(1)} custom-call(f32[1,128,128]{2,1,0:T(8,128)S(1)} %get-tuple-element.132), custom_call_target="InvertDiagBlocksLowerTriangular" | custom-call | tf_op jit(solution)/shard_map/jit(cholesky)/cholesky | solution.py:72
  623.7 11.7 %cholesky.537 = f32[128,128]{1,0:T(8,128)S(1)} custom-call(f32[128,128]{1,0:T(8,128)S(1)} %cholesky.616), custom_call_target="Cholesky" | custom-call | tf_op jit(solution)/shard_map/jit(cholesky)/cholesky | solution.py:72
  635.4 10.0 %custom-call.45 = f32[1,128,128]{1,2,0:T(8,128)S(1)} custom-call(f32[1,128,128]{2,1,0:T(8,128)S(1)} %get-tuple-element.129), custom_call_target="InvertDiagBlocksLowerTriangular" | custom-call | tf_op jit(solution)/shard_map/jit(cholesky)/cholesky | solution.py:72
  646.1 11.7 %cholesky.558 = f32[128,128]{1,0:T(8,128)S(1)} custom-call(f32[128,128]{1,0:T(8,128)S(1)} %cholesky.621), custom_call_target="Cholesky" | custom-call | tf_op jit(solution)/shard_map/jit(cholesky)/cholesky | solution.py:72
  657.9 9.8 %custom-call.46 = f32[1,128,128]{1,2,0:T(8,128)S(1)} custom-call(f32[1,128,128]{2,1,0:T(8,128)S(1)} %get-tuple-element.126), custom_call_target="InvertDiagBlocksLowerTriangular" | custom-call | tf_op jit(solution)/shard_map/jit(cholesky)/cholesky | solution.py:72
  668.3 12.1 %cholesky.575 = f32[128,128]{1,0:T(8,128)S(1)} custom-call(f32[128,128]{1,0:T(8,128)S(1)} %convolution_subtract_fusion.12), custom_call_target="Cholesky" | custom-call | tf_op jit(solution)/shard_map/jit(cholesky)/cholesky | solution.py:72
  685.7 7.9 while.16
  693.6 39.3 %custom-call.47 = f32[4,128,128]{1,2,0:T(8,128)S(1)} custom-call(f32[4,128,128]{2,1,0:T(8,128)S(1)} %get-tuple-element.51), custom_call_target="InvertDiagBlocksLowerTriangular" | custom-call | tf_op jit(solution)/shard_map/triangular_solve/custom-call.3 | solution.py:16
  745.1 6.2 collective-permute-start.8
  751.3 59.4 %collective-permute-done.9 = f32[512,512]{1,0:T(8,128)S(1)} collective-permute-done((f32[512,512]{1,0:T(8,128)S(1)}, f32[512,512]{1,0:T(8,128)S(1)}, u32[]{:S(2)}, u32[]{:S(2)}) %collective-permute-start.9) | collective-permute-done | bytes 1048608 | tf_op jit(solution)/shard_map/ppermute | solution.py:12
  811.5 10.4 %while.17 = (s32[]{:T(128)}, f32[512,512]{1,0:T(8,128)S(1)}, s32[4,2]{0,1:T(2,128)S(1)}, f32[4,128,128]{2,1,0:T(8,128)}, s32[]{:T(128)}) while((s32[]{:T(128)}, f32[512,512]{1,0:T(8,128)S(1)}, s32[4,2]{0,1:T(2,128)S(1)}, f32[4,128,128]{2,1,0:T(8,128)}, s32[]{:T(128)}) %tuple.161), condition=%wide.while_cond.clone.4, body=%wide.while_body.clone.4.sunk | while | flops 2 | bytes 132205 | solution.py:16
  821.9 40.7 %custom-call.48 = f32[4,128,128]{1,2,0:T(8,128)} custom-call(f32[4,128,128]{2,1,0:T(8,128)} %get-tuple-element.52), custom_call_target="InvertDiagBlocksLowerTriangular" | custom-call | tf_op jit(solution)/shard_map/triangular_solve/custom-call.3 | solution.py:16
  (284 shorter events, 161.0 us)
Async XLA Ops:
  7.2 56.0 %all-gather.9.cloned.1.call-start = ((), (), s32[]{:S(2)}) async-start(), calls=%async_computation | async-start | bytes 2621440 | tf_op jit(solution)/shard_map/all_gather | solution.py:56
  13.1 9.3 %copy-start.12 = (bf16[1,128,512]{2,1,0:T(8,128)(2,1)S(1)}, bf16[1,128,512]{2,1,0:T(8,128)(2,1)}, u32[]{:S(2)}) copy-start(bf16[1,128,512]{2,1,0:T(8,128)(2,1)} %param.11) | copy-start | bytes 393220
  13.7 49.4 %copy-start.13 = (f32[1,128]{1,0:T(1,128)S(1)}, f32[1,128]{1,0:T(1,128)}, u32[]{:S(2)}) copy-start(f32[1,128]{1,0:T(1,128)} %param.12) | copy-start | bytes 1540
  13.9 7.7 collective-permute-start.1
  22.4 76.5 %all-gather.11.cloned.1.call-start = ((), (), s32[]{:S(2)}) async-start(), calls=%async_computation.1 | async-start | bytes 1310720 | tf_op jit(solution)/shard_map/all_gather | solution.py:69
  22.6 6.3 collective-permute-start
  66.5 165.6 %all-gather.21.cloned.1.call-start = ((), (), s32[]{:S(2)}) async-start(), calls=%async_computation.6 | async-start | bytes 1310720 | tf_op jit(solution)/shard_map/all_gather | solution.py:70
  67.3 276.1 %all-gather.13.cloned.1.call-start = ((), (), s32[]{:S(2)}) async-start(), calls=%async_computation.2 | async-start | bytes 1310720 | tf_op jit(solution)/shard_map/all_gather | solution.py:69
  98.9 1.7 copy-start.4
  232.1 3.5 copy-start.5
  236.6 14.2 %collective-permute-start.3 = (f32[512,512]{1,0:T(8,128)S(1)}, f32[512,512]{1,0:T(8,128)S(1)}, u32[]{:S(2)}, u32[]{:S(2)}) collective-permute-start(f32[512,512]{1,0:T(8,128)S(1)} %get-tuple-element.110), channel_id=1, source_target_pairs={{4,0},{8,4},{12,8},{16,12},{20,16},{24,20},{28,24},{32,28},{36,32}... | collective-permute-start | bytes 3145736 | tf_op jit(solution)/shard_map/ppermute | solution.py:12
  243.4 64.2 %collective-permute-start.2 = (f32[128,512]{0,1:T(8,128)}, f32[128,512]{0,1:T(8,128)S(1)}, u32[]{:S(2)}, u32[]{:S(2)}) collective-permute-start(f32[128,512]{0,1:T(8,128)} %fusion.103), channel_id=1, source_target_pairs={{0,4},{4,8},{8,12},{12,16},{16,20},{20,24},{24,28},{28,32},{32,36}... | collective-permute-start | bytes 786440 | tf_op jit(solution)/shard_map/ppermute | solution.py:12
  302.6 3.4 copy-start.9
  306.5 1.2 copy-start.8
  310.2 166.1 %all-gather.15.cloned.1.call-start = ((), (), s32[]{:S(2)}) async-start(), calls=%async_computation.3 | async-start | bytes 1310720 | tf_op jit(solution)/shard_map/all_gather | solution.py:70
  310.3 16.1 %collective-permute-start.4 = (f32[512,512]{1,0:T(8,128)S(1)}, f32[512,512]{1,0:T(8,128)S(1)}, u32[]{:S(2)}, u32[]{:S(2)}) collective-permute-start(f32[512,512]{1,0:T(8,128)S(1)} %pad_maximum_fusion), channel_id=1, source_target_pairs={{4,0},{8,4},{12,8},{16,12},{20,16},{24,20},{28,24},{32,28},{36,32}... | collective-permute-start | bytes 3145736 | tf_op jit(solution)/shard_map/ppermute | solution.py:12
  327.9 271.5 %all-gather.17.cloned.1.call-start = ((), (), s32[]{:S(2)}) async-start(), calls=%async_computation.4 | async-start | bytes 1310720 | tf_op jit(solution)/shard_map/all_gather | solution.py:69
  343.4 1.7 copy-start.2
  476.3 6.1 copy-start.1
  480.0 25.9 %collective-permute-start.6 = (f32[512,512]{1,0:T(8,128)S(1)}, f32[512,512]{1,0:T(8,128)S(1)}, u32[]{:S(2)}, u32[]{:S(2)}) collective-permute-start(f32[512,512]{1,0:T(8,128)S(1)} %get-tuple-element.108), channel_id=1, source_target_pairs={{8,0},{12,4},{16,8},{20,12},{24,16},{28,20},{32,24},{36,28},{40,32... | collective-permute-start | bytes 3145736 | tf_op jit(solution)/shard_map/ppermute | solution.py:12
  486.6 77.9 %collective-permute-start.5 = (f32[128,512]{0,1:T(8,128)}, f32[128,512]{0,1:T(8,128)S(1)}, u32[]{:S(2)}, u32[]{:S(2)}) collective-permute-start(f32[128,512]{0,1:T(8,128)} %fusion.101), channel_id=1, source_target_pairs={{0,8},{4,12},{8,16},{12,20},{16,24},{20,28},{24,32},{28,36},{32,40... | collective-permute-start | bytes 786440 | tf_op jit(solution)/shard_map/ppermute | solution.py:12
  557.7 4.2 copy-start.10
  562.4 2.1 copy-start.7
  567.0 165.9 %all-gather.19.cloned.1.call-start = ((), (), s32[]{:S(2)}) async-start(), calls=%async_computation.5 | async-start | bytes 1310720 | tf_op jit(solution)/shard_map/all_gather | solution.py:70
  567.1 26.0 %collective-permute-start.7 = (f32[512,512]{1,0:T(8,128)S(1)}, f32[512,512]{1,0:T(8,128)S(1)}, u32[]{:S(2)}, u32[]{:S(2)}) collective-permute-start(f32[512,512]{1,0:T(8,128)S(1)} %pad_maximum_fusion.2), channel_id=1, source_target_pairs={{8,0},{12,4},{16,8},{20,12},{24,16},{28,20},{32,24},{36,28},{40,32... | collective-permute-start | bytes 3145736 | tf_op jit(solution)/shard_map/ppermute | solution.py:12
  599.4 1.7 copy-start.3
  732.9 6.1 copy-start
  736.6 74.1 %collective-permute-start.9 = (f32[512,512]{1,0:T(8,128)S(1)}, f32[512,512]{1,0:T(8,128)S(1)}, u32[]{:S(2)}, u32[]{:S(2)}) collective-permute-start(f32[512,512]{1,0:T(8,128)S(1)} %get-tuple-element.106), channel_id=1, source_target_pairs={{16,0},{20,4},{24,8},{28,12},{32,16},{36,20},{40,24},{44,28},{48,3... | collective-permute-start | bytes 3145736 | tf_op jit(solution)/shard_map/ppermute | solution.py:12
  740.6 131.4 %collective-permute-start.10 = (f32[512,512]{1,0:T(8,128)S(1)}, f32[512,512]{1,0:T(8,128)}, u32[]{:S(2)}, u32[]{:S(2)}) collective-permute-start(f32[512,512]{1,0:T(8,128)S(1)} %pad_maximum_fusion.4), channel_id=1, source_target_pairs={{16,0},{20,4},{24,8},{28,12},{32,16},{36,20},{40,24},{44,28},{48,3... | collective-permute-start | bytes 3145736 | tf_op jit(solution)/shard_map/ppermute | solution.py:12
  745.1 124.3 %collective-permute-start.8 = (f32[128,512]{0,1:T(8,128)}, f32[128,512]{0,1:T(8,128)S(1)}, u32[]{:S(2)}, u32[]{:S(2)}) collective-permute-start(f32[128,512]{0,1:T(8,128)} %fusion.99), channel_id=1, source_target_pairs={{0,16},{4,20},{8,24},{12,28},{16,32},{20,36},{24,40},{28,44},{32,4... | collective-permute-start | bytes 786440 | tf_op jit(solution)/shard_map/ppermute | solution.py:12
  862.6 4.2 copy-start.11
  867.3 2.1 copy-start.6
Sparse Core Ops, SparseCore 0:
  22.5 40.5 all-gather.8
  66.6 32.2 all-gather.10
  101.6 32.3 all-gather.20
  310.3 33.0 all-gather.12
  345.9 30.0 all-gather.14
  567.2 32.2 all-gather.16
  602.1 29.9 all-gather.18
where the time goes:
time: 894 us; the launch traced here: 882 us
  other arithmetic  487 us (54%)
  waiting for transfers between devices  210 us (23%)
  local copies, waits for them, and re-layouts  64.4 us (7%)
  matrix products  64.2 us (7%)
  starting transfers between devices  32 us (4%)
  between operations  23.4 us (3%)
    another operation x19, other arithmetic, tri_solve(): lax.linalg.triangular_solve(factor, right, left_side=True, lower=True)  242 us
    another operation x45, other arithmetic, shards(): factor = jnp.linalg.cholesky(full_diag)  238 us
    ppermute x11, waiting for transfers between devices, passed_along(): return lax.ppermute(block, axis, route)  124 us
    another operation x79, local copies, waits for them, and re-layouts, tri_solve(): lax.linalg.triangular_solve(factor, right, left_side=True, lower=True)  55.7 us
    all_gather x3, waiting for transfers between devices, shards(): lax.all_gather(diag_rows, 'swath', axis=0, tiled=True)  51.4 us
    another operation x42, matrix products, tri_solve(): lax.linalg.triangular_solve(factor, right, left_side=True, lower=True)  35 us
    all_gather x1, waiting for transfers between devices, shards(): shard_rows = lax.all_gather(gram_input, 'swath', axis=0, tiled=True)  34.3 us
    ppermute x11, starting transfers between devices, passed_along(): return lax.ppermute(block, axis, route)  31.4 us
  transfers between devices with their start and end apart: 18, of which 11 were waited for; matrix products, arithmetic and copies ran while one was open for 66% of the time, Pallas kernels for 0%

commit v1 on v0

v1 whole, which is shorter than its diff:
```python
import functools
import jax
import jax.numpy as jnp
from jax import lax
from jax.experimental import pallas as pl
from jax.experimental.pallas import tpu as pltpu
from jax.sharding import PartitionSpec as P

LEVELS = 3
NB = 128
WIDTH = 16
f32, bf16 = jnp.float32, jnp.bfloat16
VMEM = pl.BlockSpec(memory_space=pltpu.VMEM)
SMEM = pl.BlockSpec(memory_space=pltpu.SMEM)
PARAMS = pltpu.CompilerParams(vmem_limit_bytes=48 * 2**20)
KK, KM, MK = ((0,), (0,)), ((1,), (0,)), ((1,), (1,))


def mm(a, b, dims=KM):
    return lax.dot_general(a, b, (dims, ((), ())), preferred_element_type=f32)


def halves(x):
    high = x.astype(bf16)
    return high, (x - high.astype(f32)).astype(bf16)


def thirds(x):
    high = x.astype(bf16).astype(f32)
    rest = x - high
    mid = rest.astype(bf16).astype(f32)
    return high, mid, rest - mid


def split_dot(a, b, dims=KM):
    return mm(a[0], b[0], dims) + (mm(a[0], b[1], dims) + mm(a[1], b[0], dims))


def block_inverse(a):
    lane = lax.broadcasted_iota(jnp.int32, (WIDTH, NB), 1)
    row = lax.broadcasted_iota(jnp.int32, (WIDTH, NB), 0)
    lane_all = lax.broadcasted_iota(jnp.int32, (NB, NB), 1)
    for start in range(0, NB, WIDTH):
        stop = start + WIDTH
        p = a[start:stop, :]
        inside = (lane >= start) & (lane < stop)
        left = jnp.where(inside, 0.0, jnp.where(lane < start, -p, p))
        h, m, l = thirds(left)
        lhs = jnp.concatenate([h, h, m, h, l, m], axis=0).T.astype(bf16)
        cols = [jnp.broadcast_to(p[:, start + j : start + j + 1], (WIDTH, NB)) for j in range(WIDTH)]
        x = jnp.where(inside, jnp.where(lane - start == row, 1.0, 0.0), p)
        for j in range(WIDTH):
            c = cols[j]
            scale = 1.0 / c[j : j + 1, :]
            here = row == j

            def step(v):
                t = v[j : j + 1, :] * scale
                return jnp.where(here, t, v - c * t)

            for i in range(j + 1, WIDTH):
                cols[i] = step(cols[i])
            x = step(x)
        h, m, l = thirds(x)
        rhs = jnp.concatenate([h, m, h, l, h, m], axis=0).astype(bf16)
        a = jnp.where((lane_all >= start) & (lane_all < stop), 0.0, a) - mm(lhs, rhs)
        rows = [x]
        if start:
            rows = [a[:start]] + rows
        if stop < NB:
            rows = rows + [a[stop:]]
        a = jnp.concatenate(rows, axis=0)
    return a


def inverse_kernel(d_ref, x_ref):
    size = d_ref.shape[0]
    count = size // NB
    x_ref[...] = d_ref[...]
    for b in range(count):
        s = slice(b * NB, (b + 1) * NB)
        inv = block_inverse(x_ref[s, s])
        rows = x_ref[s, :]
        lane = lax.broadcasted_iota(jnp.int32, (NB, size), 1)
        inside = (lane >= b * NB) & (lane < (b + 1) * NB)
        left = jnp.where(lane < b * NB, -rows, rows)
        w = split_dot(halves(inv), halves(jnp.where(inside, 0.0, rows)))
        w = jnp.concatenate([inv if c == b else w[:, c * NB : (c + 1) * NB] for c in range(count)], axis=1)
        w_halves = halves(w)
        for o in [*range(b + 1, count), *range(b)]:
            os = slice(o * NB, (o + 1) * NB)
            kept = [jnp.zeros((NB, NB), f32) if c == b else x_ref[os, c * NB : (c + 1) * NB] for c in range(count)]
            x_ref[os, :] = jnp.concatenate(kept, axis=1) - split_dot(halves(left[:, os].T), w_halves)
        x_ref[s, :] = w


def inverse(d):
    size = d.shape[0]
    return pl.pallas_call(
        inverse_kernel,
        out_shape=jax.ShapeDtypeStruct(d.shape, f32),
        in_specs=[VMEM],
        out_specs=VMEM,
        compiler_params=PARAMS,
        cost_estimate=pl.CostEstimate(flops=60 * size**3, bytes_accessed=8 * size * size, transcendentals=0),
        name="inverse",
    )(d)


def weigh_kernel(total_slots, ids_ref, design_ref, process_ref, own_ref, ahead_ref):
    rows = own_ref.shape[0] // 2
    me, live_count = ids_ref[0], ids_ref[1]
    own_seen = jnp.int32(0)
    for r in range(4):
        target = ids_ref[2 + r]
        is_own = target == me
        live = (r < live_count) & (is_own | (target == me + 1))
        h = design_ref[r * rows : (r + 1) * rows, :].astype(f32)
        mean_sq = jnp.mean(h * h, axis=-1, keepdims=True)
        w = h * lax.rsqrt(4.0 * total_slots * (mean_sq + 1e-06))
        w = jnp.where(live, w, 0.0).astype(bf16)
        ahead_seen = r - own_seen

        @pl.when(is_own)
        def _():
            own_ref[pl.ds(jnp.minimum(own_seen, 1) * rows, rows), :] = w

        @pl.when(jnp.logical_not(is_own))
        def _():
            ahead_ref[pl.ds(jnp.minimum(ahead_seen, 1) * rows, rows), :] = w

        own_seen = own_seen + jnp.where(is_own, 1, 0)
    ahead_ref[2 * rows :, :] = process_ref[...]


def gram_kernel(own_ref, incoming_ref, g_ref):
    both = jnp.concatenate([own_ref[...], incoming_ref[: own_ref.shape[0], :]], axis=0)
    g_ref[...] = mm(both, both, KK)


def products_kernel(sid_ref, x_ref, q0, q1, q2, q3, left_ref, right_ref, a_full, c_full):
    sid = sid_ref[0]
    size = x_ref.shape[0]
    for k, piece in enumerate((q0, q1, q2, q3)):
        at = pl.multiple_of(lax.rem(sid - k + 4, 4) * NB, NB)
        a_full[pl.ds(at, NB), :] = piece[:NB, :].astype(f32)
        c_full[pl.ds(at, NB), :] = piece[NB:, :].astype(f32)
    col = pl.multiple_of(sid * NB, NB)
    lhs = jnp.concatenate([q0[:NB, :].astype(f32), c_full[:, pl.ds(col, NB)].T], axis=0)
    z = split_dot(halves(lhs), halves(x_ref[...]))
    zh, zl = halves(z)
    both = split_dot((zh, zl), halves(c_full[...]))
    right_term = split_dot((zh[:NB], zl[:NB]), halves(a_full[...]), MK)
    coupled = -both[:NB]
    left_ref[:NB, :] = right_term
    left_ref[NB:, :] = coupled
    right_ref[:NB, :] = both[NB:]
    right_ref[NB:, :] = coupled


def products(sid, x, pieces):
    size = x.shape[0]
    out = jax.ShapeDtypeStruct((2 * NB, size), f32)
    return pl.pallas_call(
        products_kernel,
        out_shape=(out, out),
        in_specs=[SMEM] + [VMEM] * 5,
        out_specs=(VMEM, VMEM),
        scratch_shapes=[pltpu.VMEM((size, size), f32)] * 2,
        compiler_params=PARAMS,
        cost_estimate=pl.CostEstimate(flops=4 * size**3, bytes_accessed=16 * size * size, transcendentals=0),
        name="products",
    )(sid, x, *pieces)


def passed_along(block, axis, distance, around=False):
    count = lax.axis_size(axis)
    route = [(i, (i + distance) % count) for i in range(count) if around or 0 <= i + distance < count]
    return lax.ppermute(block, axis, route)


def gathered(rows):
    copies = jnp.concatenate([rows] * lax.axis_size("swath"), axis=0)
    return lax.all_to_all(copies, "swath", 0, 0, tiled=True)


def shards(design, process, prior_prec, routes, counts):
    row_count, size = process.shape[1:]
    me = lax.axis_index("tm")
    sid = lax.axis_index("swath")
    total_slots = design.shape[1] * lax.axis_size("swath")
    ids = jnp.concatenate([me[None].astype(jnp.int32), counts[0], routes[0]])
    half = design.shape[1] // 2
    own, ahead = pl.pallas_call(
        functools.partial(weigh_kernel, total_slots),
        out_shape=(
            jax.ShapeDtypeStruct((half, size), bf16),
            jax.ShapeDtypeStruct((half + row_count, size), bf16),
        ),
        in_specs=[SMEM, VMEM, VMEM],
        out_specs=(VMEM, VMEM),
        compiler_params=PARAMS,
        name="weigh",
    )(ids, design[0], process[0])
    incoming = passed_along(ahead, "tm", 1)
    partial = pl.pallas_call(
        gram_kernel,
        out_shape=jax.ShapeDtypeStruct((size, size), f32),
        in_specs=[VMEM, VMEM],
        out_specs=VMEM,
        compiler_params=PARAMS,
        name="gram",
    )(own, incoming)
    pieces_of_gram = lax.all_to_all(partial, "swath", 0, 0, tiled=True)
    gram = jnp.sum(pieces_of_gram.reshape(-1, row_count, size), axis=0)
    previous = incoming[half:]
    unit_rows = jnp.arange(size)[None, :] == jnp.arange(row_count)[:, None] + sid * row_count
    diag_rows = previous.astype(f32) + process[0].astype(f32) + gram
    diag_rows = diag_rows + jnp.where(unit_rows, prior_prec[0][:, None], 0.0)
    pair = -jnp.concatenate([previous, process[0]], axis=0)
    sids = sid[None].astype(jnp.int32)
    for level in range(LEVELS):
        distance = 2**level
        pieces = [pair] + [passed_along(pair, "swath", k, True) for k in (1, 2, 3)]
        x = inverse(gathered(diag_rows))
        left, right = products(sids, x, pieces)
        from_right = passed_along(left, "tm", -distance)
        from_left = passed_along(right, "tm", distance)
        diag_rows = diag_rows - from_left[:row_count] - from_right[:row_count]
        pair = jnp.concatenate([from_left[row_count:], from_right[row_count:]], axis=0)
    return (diag_rows[None], pair[row_count:][None])


def solution(mesh):
    return jax.shard_map(
        shards,
        mesh=mesh,
        in_specs=(
            P("tm", "swath", None),
            P("tm", "swath", None),
            P("tm", "swath"),
            P("tm", "swath"),
            P("tm", "swath"),
        ),
        out_specs=(P("tm", "swath", None), P("tm", "swath", None)),
        check_vma=False,
    )
```

time: 894 us -> 232 us (0.26)
  the two profiles are of different devices: /device:TPU:20 before, /device:TPU:265 now
where the time goes in v1:
time: 232 us; the launch traced here: 231 us
  waiting for transfers between devices  95 us (41%)
  starting transfers between devices  74.4 us (32%)
  Pallas kernels  51.6 us (22%)
  other arithmetic  4.81 us (2%)
  local copies, waits for them, and re-layouts  3.26 us (1%)
    ppermute x16, waiting for transfers between devices, passed_along(): return lax.ppermute(block, axis, route)  71.8 us
    ppermute x16, starting transfers between devices, passed_along(): return lax.ppermute(block, axis, route)  59.8 us
    pallas_call x3, Pallas kernels, inverse(): pl.pallas_call(inverse_kernel, out_shape=jax.ShapeDtypeStruct(d.shape, f3...  43.8 us
    all_to_all x1, waiting for transfers between devices, shards(): pieces_of_gram = lax.all_to_all(partial, 'swath', 0, 0, tiled=True)  13.5 us
    all_to_all x3, starting transfers between devices, gathered(): return lax.all_to_all(copies, 'swath', 0, 0, tiled=True)  10.5 us
    all_to_all x3, waiting for transfers between devices, gathered(): return lax.all_to_all(copies, 'swath', 0, 0, tiled=True)  9.69 us
    pallas_call x3, Pallas kernels, products(): pl.pallas_call(products_kernel, out_shape=(out, out), in_specs=[SMEM] + [...  5.22 us
  transfers between devices with their start and end apart: 20, of which 13 were waited for; matrix products, arithmetic and copies ran while one was open for 0% of the time, Pallas kernels for 19%

profile of v1, /device:TPU:265, one launch (start us, length us, event | category | flops | bytes accessed | tf_op | source)
XLA Modules:
  0.0 230.7 jit_solution(17089580979832180779)
XLA Ops:
  1.3 0.6 copy-done.6
  2.0 0.9 copy-done
  2.9 1.0 copy-done.2
  4.0 1.1 weigh.1
  5.0 3.8 %collective-permute-start = (bf16[384,512]{1,0:T(8,128)(2,1)S(1)}, bf16[384,512]{1,0:T(8,128)(2,1)S(1)}, u32[]{:S(2)}, u32[]{:S(2)}) collective-permute-start(bf16[384,512]{1,0:T(8,128)(2,1)S(1)} %get-tuple-element.10), channel_id=1, source_target_pairs={{0,4},{4,8},{8,12},{12,16},{16,20},{20,24},{24,28},{28,32},{32,36}... | collective-permute-start | bytes 1179656 | tf_op jit(solution)/shard_map/ppermute | solution.py:179
  8.8 4.7 %collective-permute-done.incoming_ref = bf16[384,512]{1,0:T(8,128)(2,1)S(1)} collective-permute-done((bf16[384,512]{1,0:T(8,128)(2,1)S(1)}, bf16[384,512]{1,0:T(8,128)(2,1)S(1)}, u32[]{:S(2)}, u32[]{:S(2)}) %collective-permute-start) | collective-permute-done | bytes 393248 | tf_op jit(solution)/shard_map/ppermute | solution.py:179
  13.5 1.4 gram.1
  15.0 4.0 %all-to-all-start = ((f32[4,128,512]{2,1,0:T(8,128)}), f32[4,128,512]{2,1,0:T(8,128)S(1)}, u32[]{:S(2)}, u32[]{:S(2)}) async-start(f32[4,128,512]{2,1,0:T(8,128)} %bitcast.5), calls=%async_computation | async-start | bytes 2097152 | tf_op jit(solution)/shard_map/all_to_all | solution.py:214
  19.0 13.5 %all-to-all-done = f32[4,128,512]{2,1,0:T(8,128)S(1)} async-done(((f32[4,128,512]{2,1,0:T(8,128)}), f32[4,128,512]{2,1,0:T(8,128)S(1)}, u32[]{:S(2)}, u32[]{:S(2)}) %all-to-all-start) | async-done | bytes 1048608 | tf_op jit(solution)/shard_map/all_to_all | solution.py:214
  33.4 1.1 pad_maximum_fusion
  34.5 3.5 %all-to-all-start.1 = ((f32[4,128,512]{2,1,0:T(8,128)}), f32[4,128,512]{2,1,0:T(8,128)S(1)}, u32[]{:S(2)}, u32[]{:S(2)}) async-start(f32[4,128,512]{2,1,0:T(8,128)} %bitcast.8), calls=%async_computation.1 | async-start | bytes 2097152 | tf_op jit(solution)/shard_map/all_to_all | solution.py:184
  38.1 3.3 %collective-permute-start.1 = (bf16[256,512]{1,0:T(8,128)(2,1)S(1)}, bf16[256,512]{1,0:T(8,128)(2,1)S(1)}, u32[]{:S(2)}, u32[]{:S(2)}) collective-permute-start(bf16[256,512]{1,0:T(8,128)(2,1)S(1)} %maximum_negate_fusion.q0), channel_id=1, source_target_pairs={{0,1},{1,2},{2,3},{3,0},{4,5},{5,6},{6,7},{7,4},{8,9},{9,10},{10,1... | collective-permute-start | bytes 786440 | tf_op jit(solution)/shard_map/ppermute | solution.py:179
  41.4 4.3 %collective-permute-start.2 = (bf16[256,512]{1,0:T(8,128)(2,1)S(1)}, bf16[256,512]{1,0:T(8,128)(2,1)S(1)}, u32[]{:S(2)}, u32[]{:S(2)}) collective-permute-start(bf16[256,512]{1,0:T(8,128)(2,1)S(1)} %maximum_negate_fusion.q0), channel_id=1, source_target_pairs={{0,2},{1,3},{2,0},{3,1},{4,6},{5,7},{6,4},{7,5},{8,10},{9,11},{10,... | collective-permute-start | bytes 786440 | tf_op jit(solution)/shard_map/ppermute | solution.py:179
  45.8 3.1 %collective-permute-start.3 = (bf16[256,512]{1,0:T(8,128)(2,1)S(1)}, bf16[256,512]{1,0:T(8,128)(2,1)S(1)}, u32[]{:S(2)}, u32[]{:S(2)}) collective-permute-start(bf16[256,512]{1,0:T(8,128)(2,1)S(1)} %maximum_negate_fusion.q0), channel_id=1, source_target_pairs={{0,3},{1,0},{2,1},{3,2},{4,7},{5,4},{6,5},{7,6},{8,11},{9,8},{10,9... | collective-permute-start | bytes 786440 | tf_op jit(solution)/shard_map/ppermute | solution.py:179
  48.8 1.5 all-to-all-done.1
  50.3 14.6 %inverse.3.x_ref = f32[512,512]{1,0:T(8,128)S(1)} custom-call(f32[512,512]{1,0:T(8,128)S(1)} %bitcast.22), custom_call_target="tpu_custom_call" | custom-call | flops 8053063680 | bytes 2097152 | tf_op jit(solution)/shard_map/inverse/pallas_call | solution.py:99
  65.0 1.7 products.3
  66.7 9.9 %collective-permute-start.4 = (f32[256,512]{1,0:T(8,128)S(1)}, f32[256,512]{1,0:T(8,128)S(1)}, u32[]{:S(2)}, u32[]{:S(2)}) collective-permute-start(f32[256,512]{1,0:T(8,128)S(1)} %get-tuple-element.12), channel_id=1, source_target_pairs={{0,4},{4,8},{8,12},{12,16},{16,20},{20,24},{24,28},{28,32},{32,36}... | collective-permute-start | bytes 1572872 | tf_op jit(solution)/shard_map/ppermute | solution.py:179
  76.6 1.9 collective-permute-start.5
  78.5 4.2 %collective-permute-done.4 = f32[256,512]{1,0:T(8,128)S(1)} collective-permute-done((f32[256,512]{1,0:T(8,128)S(1)}, f32[256,512]{1,0:T(8,128)S(1)}, u32[]{:S(2)}, u32[]{:S(2)}) %collective-permute-start.4) | collective-permute-done | bytes 524320 | tf_op jit(solution)/shard_map/ppermute | solution.py:179
  82.7 4.4 %collective-permute-done.5 = f32[256,512]{1,0:T(8,128)S(1)} collective-permute-done((f32[256,512]{1,0:T(8,128)S(1)}, f32[256,512]{1,0:T(8,128)S(1)}, u32[]{:S(2)}, u32[]{:S(2)}) %collective-permute-start.5) | collective-permute-done | bytes 524320 | tf_op jit(solution)/shard_map/ppermute | solution.py:179
  87.2 1.1 pad_maximum_fusion.1
  88.3 3.5 %all-to-all-start.2 = ((f32[4,128,512]{2,1,0:T(8,128)}), f32[4,128,512]{2,1,0:T(8,128)S(1)}, u32[]{:S(2)}, u32[]{:S(2)}) async-start(f32[4,128,512]{2,1,0:T(8,128)} %bitcast.10), calls=%async_computation.2 | async-start | bytes 2097152 | tf_op jit(solution)/shard_map/all_to_all | solution.py:184
  91.9 3.3 %collective-permute-start.6 = (f32[256,512]{1,0:T(8,128)S(1)}, f32[256,512]{1,0:T(8,128)S(1)}, u32[]{:S(2)}, u32[]{:S(2)}) collective-permute-start(f32[256,512]{1,0:T(8,128)S(1)} %pad_maximum_fusion.3.q0), channel_id=1, source_target_pairs={{0,1},{1,2},{2,3},{3,0},{4,5},{5,6},{6,7},{7,4},{8,9},{9,10},{10,1... | collective-permute-start | bytes 1572872 | tf_op jit(solution)/shard_map/ppermute | solution.py:179
  95.2 4.3 %collective-permute-start.7 = (f32[256,512]{1,0:T(8,128)S(1)}, f32[256,512]{1,0:T(8,128)S(1)}, u32[]{:S(2)}, u32[]{:S(2)}) collective-permute-start(f32[256,512]{1,0:T(8,128)S(1)} %pad_maximum_fusion.3.q0), channel_id=1, source_target_pairs={{0,2},{1,3},{2,0},{3,1},{4,6},{5,7},{6,4},{7,5},{8,10},{9,11},{10,... | collective-permute-start | bytes 1572872 | tf_op jit(solution)/shard_map/ppermute | solution.py:179
  99.5 3.3 %collective-permute-start.8 = (f32[256,512]{1,0:T(8,128)S(1)}, f32[256,512]{1,0:T(8,128)S(1)}, u32[]{:S(2)}, u32[]{:S(2)}) collective-permute-start(f32[256,512]{1,0:T(8,128)S(1)} %pad_maximum_fusion.3.q0), channel_id=1, source_target_pairs={{0,3},{1,0},{2,1},{3,2},{4,7},{5,4},{6,5},{7,6},{8,11},{9,8},{10,9... | collective-permute-start | bytes 1572872 | tf_op jit(solution)/shard_map/ppermute | solution.py:179
  102.8 4.4 %all-to-all-done.2 = f32[4,128,512]{2,1,0:T(8,128)S(1)} async-done(((f32[4,128,512]{2,1,0:T(8,128)}), f32[4,128,512]{2,1,0:T(8,128)S(1)}, u32[]{:S(2)}, u32[]{:S(2)}) %all-to-all-start.2) | async-done | bytes 1048608 | tf_op jit(solution)/shard_map/all_to_all | solution.py:184
  107.2 14.6 %inverse.4.x_ref = f32[512,512]{1,0:T(8,128)S(1)} custom-call(f32[512,512]{1,0:T(8,128)S(1)} %bitcast.23), custom_call_target="tpu_custom_call" | custom-call | flops 8053063680 | bytes 2097152 | tf_op jit(solution)/shard_map/inverse/pallas_call | solution.py:99
  121.8 7.0 %collective-permute-done.7.q2 = f32[256,512]{1,0:T(8,128)S(1)} collective-permute-done((f32[256,512]{1,0:T(8,128)S(1)}, f32[256,512]{1,0:T(8,128)S(1)}, u32[]{:S(2)}, u32[]{:S(2)}) %collective-permute-start.7) | collective-permute-done | bytes 524320 | tf_op jit(solution)/shard_map/ppermute | solution.py:179
  128.8 1.7 products.4
  130.6 3.2 %collective-permute-start.9 = (f32[256,512]{1,0:T(8,128)S(1)}, f32[256,512]{1,0:T(8,128)S(1)}, u32[]{:S(2)}, u32[]{:S(2)}) collective-permute-start(f32[256,512]{1,0:T(8,128)S(1)} %get-tuple-element.14), channel_id=1, source_target_pairs={{0,8},{4,12},{8,16},{12,20},{16,24},{20,28},{24,32},{28,36},{32,40... | collective-permute-start | bytes 1572872 | tf_op jit(solution)/shard_map/ppermute | solution.py:179
  133.8 2.1 collective-permute-start.10
  135.9 10.1 %collective-permute-done.9 = f32[256,512]{1,0:T(8,128)S(1)} collective-permute-done((f32[256,512]{1,0:T(8,128)S(1)}, f32[256,512]{1,0:T(8,128)S(1)}, u32[]{:S(2)}, u32[]{:S(2)}) %collective-permute-start.9) | collective-permute-done | bytes 524320 | tf_op jit(solution)/shard_map/ppermute | solution.py:179
  146.0 4.5 %collective-permute-done.10 = f32[256,512]{1,0:T(8,128)S(1)} collective-permute-done((f32[256,512]{1,0:T(8,128)S(1)}, f32[256,512]{1,0:T(8,128)S(1)}, u32[]{:S(2)}, u32[]{:S(2)}) %collective-permute-start.10) | collective-permute-done | bytes 524320 | tf_op jit(solution)/shard_map/ppermute | solution.py:179
  150.6 1.1 pad_maximum_fusion.2
  151.7 3.5 %all-to-all-start.3 = ((f32[4,128,512]{2,1,0:T(8,128)}), f32[4,128,512]{2,1,0:T(8,128)S(1)}, u32[]{:S(2)}, u32[]{:S(2)}) async-start(f32[4,128,512]{2,1,0:T(8,128)} %bitcast.12), calls=%async_computation.3 | async-start | bytes 2097152 | tf_op jit(solution)/shard_map/all_to_all | solution.py:184
  155.3 3.3 %collective-permute-start.11 = (f32[256,512]{1,0:T(8,128)S(1)}, f32[256,512]{1,0:T(8,128)S(1)}, u32[]{:S(2)}, u32[]{:S(2)}) collective-permute-start(f32[256,512]{1,0:T(8,128)S(1)} %pad_maximum_fusion.4.q0), channel_id=1, source_target_pairs={{0,1},{1,2},{2,3},{3,0},{4,5},{5,6},{6,7},{7,4},{8,9},{9,10},{10,1... | collective-permute-start | bytes 1572872 | tf_op jit(solution)/shard_map/ppermute | solution.py:179
  158.6 4.3 %collective-permute-start.12 = (f32[256,512]{1,0:T(8,128)S(1)}, f32[256,512]{1,0:T(8,128)S(1)}, u32[]{:S(2)}, u32[]{:S(2)}) collective-permute-start(f32[256,512]{1,0:T(8,128)S(1)} %pad_maximum_fusion.4.q0), channel_id=1, source_target_pairs={{0,2},{1,3},{2,0},{3,1},{4,6},{5,7},{6,4},{7,5},{8,10},{9,11},{10,... | collective-permute-start | bytes 1572872 | tf_op jit(solution)/shard_map/ppermute | solution.py:179
  162.9 3.3 %collective-permute-start.13 = (f32[256,512]{1,0:T(8,128)S(1)}, f32[256,512]{1,0:T(8,128)S(1)}, u32[]{:S(2)}, u32[]{:S(2)}) collective-permute-start(f32[256,512]{1,0:T(8,128)S(1)} %pad_maximum_fusion.4.q0), channel_id=1, source_target_pairs={{0,3},{1,0},{2,1},{3,2},{4,7},{5,4},{6,5},{7,6},{8,11},{9,8},{10,9... | collective-permute-start | bytes 1572872 | tf_op jit(solution)/shard_map/ppermute | solution.py:179
  166.2 3.8 %all-to-all-done.3 = f32[4,128,512]{2,1,0:T(8,128)S(1)} async-done(((f32[4,128,512]{2,1,0:T(8,128)}), f32[4,128,512]{2,1,0:T(8,128)S(1)}, u32[]{:S(2)}, u32[]{:S(2)}) %all-to-all-start.3) | async-done | bytes 1048608 | tf_op jit(solution)/shard_map/all_to_all | solution.py:184
  170.1 14.6 %inverse.5.x_ref = f32[512,512]{1,0:T(8,128)S(1)} custom-call(f32[512,512]{1,0:T(8,128)S(1)} %bitcast.24), custom_call_target="tpu_custom_call" | custom-call | flops 8053063680 | bytes 2097152 | tf_op jit(solution)/shard_map/inverse/pallas_call | solution.py:99
  184.7 7.8 %collective-permute-done.12.q2 = f32[256,512]{1,0:T(8,128)S(1)} collective-permute-done((f32[256,512]{1,0:T(8,128)S(1)}, f32[256,512]{1,0:T(8,128)S(1)}, u32[]{:S(2)}, u32[]{:S(2)}) %collective-permute-start.12) | collective-permute-done | bytes 524320 | tf_op jit(solution)/shard_map/ppermute | solution.py:179
  192.5 1.8 products.5
  194.3 4.5 %collective-permute-start.15 = (f32[256,512]{1,0:T(8,128)S(1)}, f32[256,512]{1,0:T(8,128)S(1)}, u32[]{:S(2)}, u32[]{:S(2)}) collective-permute-start(f32[256,512]{1,0:T(8,128)S(1)} %get-tuple-element.17), channel_id=1, source_target_pairs={{16,0},{20,4},{24,8},{28,12},{32,16},{36,20},{40,24},{44,28},{48,3... | collective-permute-start | bytes 1572872 | tf_op jit(solution)/shard_map/ppermute | solution.py:179
  198.8 1.9 collective-permute-start.14
  200.7 19.3 %collective-permute-done.15 = f32[256,512]{1,0:T(8,128)S(1)} collective-permute-done((f32[256,512]{1,0:T(8,128)S(1)}, f32[256,512]{1,0:T(8,128)S(1)}, u32[]{:S(2)}, u32[]{:S(2)}) %collective-permute-start.15) | collective-permute-done | bytes 524320 | tf_op jit(solution)/shard_map/ppermute | solution.py:179
  220.0 9.8 %collective-permute-done.14 = f32[256,512]{1,0:T(8,128)S(1)} collective-permute-done((f32[256,512]{1,0:T(8,128)S(1)}, f32[256,512]{1,0:T(8,128)S(1)}, u32[]{:S(2)}, u32[]{:S(2)}) %collective-permute-start.14) | collective-permute-done | bytes 524320 | tf_op jit(solution)/shard_map/ppermute | solution.py:179
  229.8 0.9 slice_bitcast_fusion
  (28 shorter events, 1.3 us)
Async XLA Ops:
  1.3 0.7 copy-start.6
  2.0 0.9 copy-start
  2.9 1.0 copy-start.2
  5.0 8.5 %collective-permute-start = (bf16[384,512]{1,0:T(8,128)(2,1)S(1)}, bf16[384,512]{1,0:T(8,128)(2,1)S(1)}, u32[]{:S(2)}, u32[]{:S(2)}) collective-permute-start(bf16[384,512]{1,0:T(8,128)(2,1)S(1)} %get-tuple-element.10), channel_id=1, source_target_pairs={{0,4},{4,8},{8,12},{12,16},{16,20},{20,24},{24,28},{28,32},{32,36}... | collective-permute-start | bytes 1179656 | tf_op jit(solution)/shard_map/ppermute | solution.py:179
  15.0 17.6 %all-to-all-start = ((f32[4,128,512]{2,1,0:T(8,128)}), f32[4,128,512]{2,1,0:T(8,128)S(1)}, u32[]{:S(2)}, u32[]{:S(2)}) async-start(f32[4,128,512]{2,1,0:T(8,128)} %bitcast.5), calls=%async_computation | async-start | bytes 2097152 | tf_op jit(solution)/shard_map/all_to_all | solution.py:214
  19.0 13.6 %copy-start.1 = (bf16[1,128,512]{2,1,0:T(8,128)(2,1)S(1)}, bf16[1,128,512]{2,1,0:T(8,128)(2,1)}, u32[]{:S(2)}) copy-start(bf16[1,128,512]{2,1,0:T(8,128)(2,1)} %param.6) | copy-start | bytes 393220
  32.6 0.7 copy-start.5
  34.5 15.8 %all-to-all-start.1 = ((f32[4,128,512]{2,1,0:T(8,128)}), f32[4,128,512]{2,1,0:T(8,128)S(1)}, u32[]{:S(2)}, u32[]{:S(2)}) async-start(f32[4,128,512]{2,1,0:T(8,128)} %bitcast.8), calls=%async_computation.1 | async-start | bytes 2097152 | tf_op jit(solution)/shard_map/all_to_all | solution.py:184
  38.1 26.8 %collective-permute-start.1 = (bf16[256,512]{1,0:T(8,128)(2,1)S(1)}, bf16[256,512]{1,0:T(8,128)(2,1)S(1)}, u32[]{:S(2)}, u32[]{:S(2)}) collective-permute-start(bf16[256,512]{1,0:T(8,128)(2,1)S(1)} %maximum_negate_fusion.q0), channel_id=1, source_target_pairs={{0,1},{1,2},{2,3},{3,0},{4,5},{5,6},{6,7},{7,4},{8,9},{9,10},{10,1... | collective-permute-start | bytes 786440 | tf_op jit(solution)/shard_map/ppermute | solution.py:179
  41.4 23.5 %collective-permute-start.2 = (bf16[256,512]{1,0:T(8,128)(2,1)S(1)}, bf16[256,512]{1,0:T(8,128)(2,1)S(1)}, u32[]{:S(2)}, u32[]{:S(2)}) collective-permute-start(bf16[256,512]{1,0:T(8,128)(2,1)S(1)} %maximum_negate_fusion.q0), channel_id=1, source_target_pairs={{0,2},{1,3},{2,0},{3,1},{4,6},{5,7},{6,4},{7,5},{8,10},{9,11},{10,... | collective-permute-start | bytes 786440 | tf_op jit(solution)/shard_map/ppermute | solution.py:179
  45.8 19.2 %collective-permute-start.3 = (bf16[256,512]{1,0:T(8,128)(2,1)S(1)}, bf16[256,512]{1,0:T(8,128)(2,1)S(1)}, u32[]{:S(2)}, u32[]{:S(2)}) collective-permute-start(bf16[256,512]{1,0:T(8,128)(2,1)S(1)} %maximum_negate_fusion.q0), channel_id=1, source_target_pairs={{0,3},{1,0},{2,1},{3,2},{4,7},{5,4},{6,5},{7,6},{8,11},{9,8},{10,9... | collective-permute-start | bytes 786440 | tf_op jit(solution)/shard_map/ppermute | solution.py:179
  66.7 16.0 %collective-permute-start.4 = (f32[256,512]{1,0:T(8,128)S(1)}, f32[256,512]{1,0:T(8,128)S(1)}, u32[]{:S(2)}, u32[]{:S(2)}) collective-permute-start(f32[256,512]{1,0:T(8,128)S(1)} %get-tuple-element.12), channel_id=1, source_target_pairs={{0,4},{4,8},{8,12},{12,16},{16,20},{20,24},{24,28},{28,32},{32,36}... | collective-permute-start | bytes 1572872 | tf_op jit(solution)/shard_map/ppermute | solution.py:179
  76.6 10.5 %collective-permute-start.5 = (f32[256,512]{1,0:T(8,128)S(1)}, f32[256,512]{1,0:T(8,128)S(1)}, u32[]{:S(2)}, u32[]{:S(2)}) collective-permute-start(f32[256,512]{1,0:T(8,128)S(1)} %get-tuple-element.13), channel_id=1, source_target_pairs={{4,0},{8,4},{12,8},{16,12},{20,16},{24,20},{28,24},{32,28},{36,32}... | collective-permute-start | bytes 1572872 | tf_op jit(solution)/shard_map/ppermute | solution.py:179
  87.2 1.1 copy-start.3
  88.3 18.9 %all-to-all-start.2 = ((f32[4,128,512]{2,1,0:T(8,128)}), f32[4,128,512]{2,1,0:T(8,128)S(1)}, u32[]{:S(2)}, u32[]{:S(2)}) async-start(f32[4,128,512]{2,1,0:T(8,128)} %bitcast.10), calls=%async_computation.2 | async-start | bytes 2097152 | tf_op jit(solution)/shard_map/all_to_all | solution.py:184
  91.9 29.9 %collective-permute-start.6 = (f32[256,512]{1,0:T(8,128)S(1)}, f32[256,512]{1,0:T(8,128)S(1)}, u32[]{:S(2)}, u32[]{:S(2)}) collective-permute-start(f32[256,512]{1,0:T(8,128)S(1)} %pad_maximum_fusion.3.q0), channel_id=1, source_target_pairs={{0,1},{1,2},{2,3},{3,0},{4,5},{5,6},{6,7},{7,4},{8,9},{9,10},{10,1... | collective-permute-start | bytes 1572872 | tf_op jit(solution)/shard_map/ppermute | solution.py:179
  95.2 33.6 %collective-permute-start.7 = (f32[256,512]{1,0:T(8,128)S(1)}, f32[256,512]{1,0:T(8,128)S(1)}, u32[]{:S(2)}, u32[]{:S(2)}) collective-permute-start(f32[256,512]{1,0:T(8,128)S(1)} %pad_maximum_fusion.3.q0), channel_id=1, source_target_pairs={{0,2},{1,3},{2,0},{3,1},{4,6},{5,7},{6,4},{7,5},{8,10},{9,11},{10,... | collective-permute-start | bytes 1572872 | tf_op jit(solution)/shard_map/ppermute | solution.py:179
  99.5 29.3 %collective-permute-start.8 = (f32[256,512]{1,0:T(8,128)S(1)}, f32[256,512]{1,0:T(8,128)S(1)}, u32[]{:S(2)}, u32[]{:S(2)}) collective-permute-start(f32[256,512]{1,0:T(8,128)S(1)} %pad_maximum_fusion.3.q0), channel_id=1, source_target_pairs={{0,3},{1,0},{2,1},{3,2},{4,7},{5,4},{6,5},{7,6},{8,11},{9,8},{10,9... | collective-permute-start | bytes 1572872 | tf_op jit(solution)/shard_map/ppermute | solution.py:179
  121.8 28.7 %copy-start.4 = (f32[128,512]{1,0:T(8,128)S(1)}, f32[128,512]{1,0:T(8,128)}, u32[]{:S(2)}) copy-start(f32[128,512]{1,0:T(8,128)} %copy-done.3) | copy-start | bytes 786436
  130.6 15.4 %collective-permute-start.9 = (f32[256,512]{1,0:T(8,128)S(1)}, f32[256,512]{1,0:T(8,128)S(1)}, u32[]{:S(2)}, u32[]{:S(2)}) collective-permute-start(f32[256,512]{1,0:T(8,128)S(1)} %get-tuple-element.14), channel_id=1, source_target_pairs={{0,8},{4,12},{8,16},{12,20},{16,24},{20,28},{24,32},{28,36},{32,40... | collective-permute-start | bytes 1572872 | tf_op jit(solution)/shard_map/ppermute | solution.py:179
  133.8 16.7 %collective-permute-start.10 = (f32[256,512]{1,0:T(8,128)S(1)}, f32[256,512]{1,0:T(8,128)S(1)}, u32[]{:S(2)}, u32[]{:S(2)}) collective-permute-start(f32[256,512]{1,0:T(8,128)S(1)} %get-tuple-element.15), channel_id=1, source_target_pairs={{8,0},{12,4},{16,8},{20,12},{24,16},{28,20},{32,24},{36,28},{40,32... | collective-permute-start | bytes 1572872 | tf_op jit(solution)/shard_map/ppermute | solution.py:179
  151.7 18.4 %all-to-all-start.3 = ((f32[4,128,512]{2,1,0:T(8,128)}), f32[4,128,512]{2,1,0:T(8,128)S(1)}, u32[]{:S(2)}, u32[]{:S(2)}) async-start(f32[4,128,512]{2,1,0:T(8,128)} %bitcast.12), calls=%async_computation.3 | async-start | bytes 2097152 | tf_op jit(solution)/shard_map/all_to_all | solution.py:184
  155.3 29.4 %collective-permute-start.11 = (f32[256,512]{1,0:T(8,128)S(1)}, f32[256,512]{1,0:T(8,128)S(1)}, u32[]{:S(2)}, u32[]{:S(2)}) collective-permute-start(f32[256,512]{1,0:T(8,128)S(1)} %pad_maximum_fusion.4.q0), channel_id=1, source_target_pairs={{0,1},{1,2},{2,3},{3,0},{4,5},{5,6},{6,7},{7,4},{8,9},{9,10},{10,1... | collective-permute-start | bytes 1572872 | tf_op jit(solution)/shard_map/ppermute | solution.py:179
  158.6 33.9 %collective-permute-start.12 = (f32[256,512]{1,0:T(8,128)S(1)}, f32[256,512]{1,0:T(8,128)S(1)}, u32[]{:S(2)}, u32[]{:S(2)}) collective-permute-start(f32[256,512]{1,0:T(8,128)S(1)} %pad_maximum_fusion.4.q0), channel_id=1, source_target_pairs={{0,2},{1,3},{2,0},{3,1},{4,6},{5,7},{6,4},{7,5},{8,10},{9,11},{10,... | collective-permute-start | bytes 1572872 | tf_op jit(solution)/shard_map/ppermute | solution.py:179
  162.9 29.6 %collective-permute-start.13 = (f32[256,512]{1,0:T(8,128)S(1)}, f32[256,512]{1,0:T(8,128)S(1)}, u32[]{:S(2)}, u32[]{:S(2)}) collective-permute-start(f32[256,512]{1,0:T(8,128)S(1)} %pad_maximum_fusion.4.q0), channel_id=1, source_target_pairs={{0,3},{1,0},{2,1},{3,2},{4,7},{5,4},{6,5},{7,6},{8,11},{9,8},{10,9... | collective-permute-start | bytes 1572872 | tf_op jit(solution)/shard_map/ppermute | solution.py:179
  194.3 25.7 %collective-permute-start.15 = (f32[256,512]{1,0:T(8,128)S(1)}, f32[256,512]{1,0:T(8,128)S(1)}, u32[]{:S(2)}, u32[]{:S(2)}) collective-permute-start(f32[256,512]{1,0:T(8,128)S(1)} %get-tuple-element.17), channel_id=1, source_target_pairs={{16,0},{20,4},{24,8},{28,12},{32,16},{36,20},{40,24},{44,28},{48,3... | collective-permute-start | bytes 1572872 | tf_op jit(solution)/shard_map/ppermute | solution.py:179
  198.8 31.0 %collective-permute-start.14 = (f32[256,512]{1,0:T(8,128)S(1)}, f32[256,512]{1,0:T(8,128)S(1)}, u32[]{:S(2)}, u32[]{:S(2)}) collective-permute-start(f32[256,512]{1,0:T(8,128)S(1)} %get-tuple-element.16), channel_id=1, source_target_pairs={{0,16},{4,20},{8,24},{12,28},{16,32},{20,36},{24,40},{28,44},{32,4... | collective-permute-start | bytes 1572872 | tf_op jit(solution)/shard_map/ppermute | solution.py:179
